TPU v7x, 32 devices: a whole 2x2x4 slice. The times are simulated.
32 devices in a mesh: tile: 8 (over z, y), sta: 4 (over x, core).
Axes of the slice: x: 2, y: 2, z: 4, core: 2. Of those that a mesh axis runs over, the one named last changes fastest.
Arguments:
- waves: bfloat16 [128, 64, 3, 512], P('sta', 'tile'), may hold values from -256 to 256
- valid: int32 [128, 64], P('sta', 'tile'), may hold values 0 or 1
- station_group: int32 [128], P('sta'), may hold values from 0 to 7, as said below
- owners: int32 [4], replicated, may hold values from 0 to 7, as said below
Outputs:
- peak: float32 [8, 32, 64], P(None, None, 'tile')
Inputs may be any that keep to these rules, and one draw needn't show every extreme that they name: `station_group`: every subnetwork holds exactly 16 stations. `owners`: distinct numbers of blocks of 8 consecutive catalog events; the last block is always among them.
All inputs are finite; a program needn't handle non-finite values. No bound on the sum of `valid` on one device may be relied on, other than what follows from the above.
Results may differ from a plain program's by a relative error of at most 0.00037.
Values may be sent and summed in bfloat16 or wider, within the bound.
A program may use at most 64 MiB of HBM per device.

v0:
```python
import jax
import jax.numpy as jnp
from jax import lax
from jax.sharding import PartitionSpec as P

SAMPLES = 512
LAGS = 64
SUB = 16
GROUPS = 8


epsilon = 1e-06
station_pass = 4


def from_root(array, axis, root):
    mine = lax.axis_index(axis) == root
    return lax.psum(jnp.where(mine, array, jnp.zeros_like(array)), axis)


def normalize(raw_block, mask_block):
    signal = raw_block.astype(jnp.float32)
    inverse_rms = lax.rsqrt(jnp.mean(signal * signal, axis=-1, keepdims=True) + epsilon)
    return (signal * inverse_rms * mask_block[:, :, None, None].astype(jnp.float32)).astype(
        jnp.bfloat16
    )


def flatten(copies):
    layout = copies.shape
    merged = copies.reshape(layout[0], layout[1] * layout[2], layout[3] * layout[4])
    padding = -merged.shape[-1] % 128
    return jnp.pad(merged, ((0, 0), (0, 0), (0, padding)))


def shifted_local(station_block):
    padded = jnp.pad(station_block, ((0, 0), (0, 0), (0, 0), (SUB, SUB)))
    length = station_block.shape[-1] + SUB
    copies = jnp.stack(
        [padded[:, :, :, SUB - offset : SUB - offset + length] for offset in range(SUB)], axis=2
    )
    return flatten(copies)


def shifted_query(station_block):
    half_lags = LAGS // 2
    padded = jnp.pad(station_block, ((0, 0), (0, 0), (0, 0), (half_lags, half_lags)))
    length = station_block.shape[-1] + SUB
    copies = jnp.stack(
        [padded[:, :, :, SUB * offset : SUB * offset + length] for offset in range(LAGS // SUB)],
        axis=2,
    )
    return flatten(copies)


def correlate(normed, queries, onehot):
    passes = normed.shape[0] // station_pass
    width_rows = queries.shape[1] * (LAGS // SUB)
    width_cols = normed.shape[1] * SUB

    def regroup(array):
        return array.reshape((passes, station_pass) + array.shape[1:])

    def accumulate(running, inputs):
        local_block, query_block, onehot_block = inputs
        products = jnp.einsum(
            "sxk,syk->sxy",
            shifted_query(query_block),
            shifted_local(local_block),
            preferred_element_type=jnp.float32,
        )
        added = jnp.einsum("sg,sxy->gxy", onehot_block, products, precision=lax.Precision.HIGHEST)
        return (running + added, None)

    initial = jnp.zeros((GROUPS, width_rows, width_cols), jnp.float32)
    return lax.scan(accumulate, initial, (regroup(normed), regroup(queries), regroup(onehot)))[0]


def group_peaks(summed, counts):
    group_count, query_count, event_count = counts.shape
    curves = summed.reshape(group_count, query_count, LAGS // SUB, event_count, SUB)
    largest = jnp.max(curves, axis=(2, 4))
    return largest / (SAMPLES * jnp.maximum(counts, 1.0))


def shards(waves, valid, station_group, owners):
    normed = normalize(waves, valid)
    sent_valid = valid.astype(jnp.bfloat16)
    onehot = (station_group[:, None] == jnp.arange(GROUPS, dtype=jnp.int32)[None, :]).astype(
        jnp.float32
    )
    blocks = owners.shape[0]

    def fetch_block(number):
        return (
            from_root(normed, "tile", owners[number]),
            from_root(sent_valid, "tile", owners[number]),
        )

    received = [fetch_block(number) for number in range(blocks)]
    queries = jnp.concatenate([pair_in[0] for pair_in in received], axis=1)
    query_valid = jnp.concatenate([pair_in[1] for pair_in in received], axis=1)
    totals = correlate(normed, queries, onehot)
    common = jnp.einsum(
        "sg,sq,se->gqe",
        onehot,
        query_valid.astype(jnp.float32),
        valid.astype(jnp.float32),
        precision=lax.Precision.HIGHEST,
    )
    summed, counts = lax.psum((totals, common), "sta")
    return group_peaks(summed, counts)


def solution(mesh):
    return jax.shard_map(
        shards,
        mesh=mesh,
        in_specs=(P("sta", "tile", None, None), P("sta", "tile"), P("sta"), P()),
        out_specs=P(None, None, "tile"),
        check_vma=False,
    )
```

profile of v0, /device:TPU:0, one launch (start us, length us, event | category | flops | bytes accessed | tf_op | source)
XLA Modules:
  0.0 397.3 jit_solution(18241895711891235174)
XLA Ops:
  17.6 132.3 %all-reduce.11.cloned.1.call-done = (bf16[32,8,3,512]{3,1,2,0:T(8,128)(2,1)}, bf16[32,8,3,512]{3,1,2,0:T(8,128)(2,1)}, bf16[32,8,3,512]{3,1,2,0:T(8,128)(2,1)}, bf16[32,8,3,512]{3,1,2,0:T(8,128)(2,1)}) async-done(((bf16[32,8,3,512]{3,1,2,0:T(8,128)(2,1)}, bf16[32,8,3,512]{3,1,2,0:T(8,128)(2,1)}, bf16[32,8,3,512]{3,1,2,0:T(8,128)(2,1)}, bf16[32,8,3,512]{3,1,2,0:T(8,128)(2,1)}), ...) | async-done | bytes 3145744 | tf_op jit(solution)/shard_map/psum | solution.py:18
  152.0 4.9 %copy.109 = bf16[32,32,3,512]{3,2,1,0:T(4,128)(2,1)} copy(bf16[32,32,3,512]{3,1,2,0:T(8,128)(2,1)S(1)} %pad_maximum_fusion.1) | data formatting | bytes 6291456 | tf_op jit(solution)/shard_map/concatenate | solution.py:101
  156.9 142.5 %while.13 = (s32[]{:T(128)}, f32[8,128,128]{2,0,1:T(8,128)S(1)}, f32[8,4,8]{2,1,0:T(4,128)S(1)}, bf16[8,4,32,3,512]{4,3,2,1,0:T(4,128)(2,1)}, bf16[8,4,8,3,512]{4,3,2,1,0:T(4,128)(2,1)S(1)}, /*index=5*/s32[]{:T(128)}, s32[]{:T(128)}) while((s32[]{:T(128)}, f32[8,128,128]{2,0,1:T(8,128)S(1)}, f32[8,4,8]{2,1,0:T(4,128)S(1)}, ...), condition=%wide.region_6.7_spmd.clone, body=%wide.region_5.6_spmd.clone.sunk | while | flops 227090432 | bytes 28526744 | solution.py:76
  160.8 2.7 reshape.50
  168.5 2.6 reshape.51
  171.1 2.7 fusion.35
  178.6 2.7 reshape.50
  186.3 2.6 reshape.51
  189.0 2.7 fusion.35
  196.5 2.7 reshape.50
  206.8 2.7 fusion.35
  214.3 2.7 reshape.50
  224.6 2.7 fusion.35
  232.1 2.7 reshape.50
  242.4 2.7 fusion.35
  249.9 2.7 reshape.50
  260.2 2.7 fusion.35
  267.7 2.7 reshape.50
  278.0 2.7 fusion.35
  285.5 2.7 reshape.50
  295.9 2.7 fusion.35
  302.2 35.1 %all-reduce.4 = (bf16[32,8]{1,0:T(8,128)(2,1)S(1)}, bf16[32,8]{1,0:T(8,128)(2,1)S(1)}, bf16[32,8]{1,0:T(8,128)(2,1)S(1)}, bf16[32,8]{1,0:T(8,128)(2,1)S(1)}) all-reduce(bf16[32,8]{1,0:T(8,128)(2,1)S(1)} %get-tuple-element.120, bf16[32,8]{1,0:T(8,128)(2,1)S(1)} %get-tuple-element.119, ...), channel_id=1, replica_groups=mesh['tile'=8,'sta'=4] {'tile'}, use_global_device_ids=true, to_apply=%region_12.13 | all-reduce | flops 1024 | bytes 4096 | tf_op jit(solution)/shard_map/psum | solution.py:18
  337.6 10.7 %psum.79 = f32[8,32,8]{1,0,2:T(8,128)S(1)} all-reduce(f32[8,32,8]{1,0,2:T(8,128)S(1)} %convolution_bitcast_fusion), channel_id=1, replica_groups=mesh['tile'=8,'sta'=4] {'sta'}, use_global_device_ids=true, to_apply=%region_13.14 | all-reduce | flops 2048 | bytes 16384 | tf_op jit(solution)/shard_map/psum | solution.py:111
  348.3 38.9 %all-reduce.9.cloned.1.call-done = f32[8,32,4,8,16]{4,3,2,1,0:T(8,128)} async-done(((f32[8,32,4,8,16]{4,3,2,1,0:T(8,128)}), f32[8,32,4,8,16]{4,3,2,1,0:T(8,128)}) %all-reduce.9.cloned.1.call-update) | async-done | bytes 524304 | tf_op jit(solution)/shard_map/psum | solution.py:111
  (239 shorter events, 110.0 us)
Async XLA Ops:
  6.5 143.4 %all-reduce.11.cloned.1.call-start = ((), (), s32[]{:S(2)}) async-start(), calls=%async_computation.1 | async-start | bytes 6291456 | tf_op jit(solution)/shard_map/psum | solution.py:18
  16.6 0.7 copy-start.2
  16.6 0.8 copy-start.3
  16.7 370.5 %all-reduce.9.cloned.1.call-start = ((), (), s32[]{:S(2)}) async-start(), calls=%async_computation | async-start | bytes 8388608 | tf_op jit(solution)/shard_map/psum | solution.py:111
  156.9 1.0 copy-start
  171.1 3.6 copy-start.1
  174.7 1.0 copy-start
  189.0 3.6 copy-start.1
  192.6 1.0 copy-start
  206.8 3.6 copy-start.1
  210.4 1.0 copy-start
  224.6 3.6 copy-start.1
  228.2 1.0 copy-start
  242.4 3.6 copy-start.1
  246.0 1.0 copy-start
  260.2 3.6 copy-start.1
  263.8 1.0 copy-start
  278.0 3.6 copy-start.1
  281.7 1.0 copy-start
  295.9 3.6 copy-start.1
Sparse Core Ops, SparseCore 0:
  16.8 133.0 all-reduce.10
  302.3 84.8 all-reduce.8
where the time goes:
time: 398 us; the launch traced here: 397 us
  waiting for transfers between devices  171 us (43%)
  local copies, waits for them, and re-layouts  105 us (26%)
  blocking collectives  45.8 us (12%)
  other arithmetic  29 us (7%)
  matrix products  28.7 us (7%)
  between operations  16 us (4%)
    psum x1, waiting for transfers between devices, from_root(): return lax.psum(jnp.where(mine, array, jnp.zeros_like(array)), axis)  132 us
    reshape x16, local copies, waits for them, and re-layouts, flatten(): copies.reshape(layout[0], layout[1] * layout[2], layout[3] * layout[4])  42.4 us
    psum x1, waiting for transfers between devices, shards(): summed, counts = lax.psum((totals, common), 'sta')  38.9 us
    psum x1, blocking collectives, from_root(): return lax.psum(jnp.where(mine, array, jnp.zeros_like(array)), axis)  35.1 us
    while x152, local copies, waits for them, and re-layouts  28.8 us
    dot_general x8, matrix products, accumulate(): jnp.einsum('sxk,syk->sxy', shifted_query(query_block), shifted_local(loca...  21.5 us
    another operation x8, other arithmetic, shifted_query(): jnp.stack([padded[:, :, :, SUB * offset:SUB * offset + length] for offset...  18.4 us
    another operation x8, local copies, waits for them, and re-layouts, shifted_query(): jnp.stack([padded[:, :, :, SUB * offset:SUB * offset + length] for offset...  11.8 us
  transfers between devices with their start and end apart: 2, of which 2 were waited for; matrix products, arithmetic and copies ran while one was open for 0% of the time, Pallas kernels for 0%

commit v1 on v0

v1 whole, which is shorter than its diff:
```python
import functools

import jax
import jax.numpy as jnp
from jax import lax
from jax.experimental import pallas as pl
from jax.experimental.pallas import tpu as pltpu
from jax.sharding import PartitionSpec as P

LAGS = 64
GROUPS = 8
PAIR = 2
CHUNK = 2
epsilon = 1e-06
MESH = pl.DeviceIdType.MESH
VMEM_LIMIT = 56 * 1024 * 1024


def normalize(raw_block, mask_block):
    signal = raw_block.astype(jnp.float32)
    inverse_rms = lax.rsqrt(jnp.mean(signal * signal, axis=-1, keepdims=True) + epsilon)
    return (signal * inverse_rms * mask_block[:, :, None, None].astype(jnp.float32)).astype(
        jnp.bfloat16
    )


def spread_kernel(
    line, slots, owners_ref, mine_ref, out_ref,
    beside, up_out, up_in, down_out, down_in,
    beside_send, beside_recv, up_send, up_recv, down_send, down_recv, out_send, out_recv,
):
    tile, sta = lax.axis_index("tile"), lax.axis_index("sta")
    layer, side = tile // 2, tile % 2
    other = layer * 2 + (1 - side)
    half = mine_ref.shape[0] // 2
    steps = half // CHUNK
    above, below = layer * 2 + 2 + side, layer * 2 - 2 + side
    has_above, has_below = layer < line - 1, layer > 0

    barrier = pltpu.get_barrier_semaphore()
    pl.semaphore_signal(barrier, inc=1, device_id=(other, sta), device_id_type=MESH)

    @pl.when(has_above)
    def _():
        pl.semaphore_signal(barrier, inc=1, device_id=(above, sta), device_id_type=MESH)

    @pl.when(has_below)
    def _():
        pl.semaphore_signal(barrier, inc=1, device_id=(below, sta), device_id_type=MESH)

    pl.semaphore_wait(
        barrier, 1 + has_above.astype(jnp.int32) + has_below.astype(jnp.int32)
    )

    def beside_copy(step):
        return pltpu.make_async_remote_copy(
            src_ref=mine_ref.at[pl.ds((1 - side) * half + step * CHUNK, CHUNK)],
            dst_ref=beside.at[step],
            send_sem=beside_send.at[step], recv_sem=beside_recv.at[step],
            device_id=(other, sta), device_id_type=MESH,
        )

    def up_copy(step):
        return pltpu.make_async_remote_copy(
            src_ref=up_out.at[step], dst_ref=up_in.at[step],
            send_sem=up_send.at[step], recv_sem=up_recv.at[step],
            device_id=(above, sta), device_id_type=MESH,
        )

    def down_copy(step):
        return pltpu.make_async_remote_copy(
            src_ref=down_out.at[step], dst_ref=down_in.at[step],
            send_sem=down_send.at[step], recv_sem=down_recv.at[step],
            device_id=(below, sta), device_id_type=MESH,
        )

    def out_copy(step, of_side):
        rows = pl.ds(of_side * half + step * CHUNK, CHUNK)
        return pltpu.make_async_remote_copy(
            src_ref=out_ref.at[:, rows], dst_ref=out_ref.at[:, rows],
            send_sem=out_send.at[step], recv_sem=out_recv.at[step],
            device_id=(other, sta), device_id_type=MESH,
        )

    def each(count, body):
        def run(index, carry):
            body(index)
            return carry

        lax.fori_loop(0, count, run, 0)

    each(steps, lambda step: beside_copy(step).start())
    own = [owners_ref[slot] == tile for slot in range(slots)]
    near = [owners_ref[slot] == other for slot in range(slots)]
    lower = [owners_ref[slot] < layer * 2 for slot in range(slots)]

    def merged(step, slot, passing):
        local = mine_ref[pl.ds(side * half + step * CHUNK, CHUNK)]
        return jnp.where(own[slot], local, jnp.where(near[slot], beside[step], passing))

    lag_up, lag_down = layer, line - 1 - layer
    lag_out = jnp.maximum(lag_up, lag_down)

    def tick(now):
        @pl.when(now < steps)
        def _():
            beside_copy(now).wait_recv()

        step_up = now - lag_up

        @pl.when(jnp.logical_and(step_up >= 0, step_up < steps))
        def _():
            @pl.when(has_below)
            def _():
                up_copy(step_up).wait_recv()

            @pl.when(has_above)
            def _():
                for slot in range(slots):
                    up_out[step_up, slot] = merged(step_up, slot, up_in[step_up, slot])
                up_copy(step_up).start()

        step_down = now - lag_down

        @pl.when(jnp.logical_and(step_down >= 0, step_down < steps))
        def _():
            @pl.when(has_above)
            def _():
                down_copy(step_down).wait_recv()

            @pl.when(has_below)
            def _():
                for slot in range(slots):
                    down_out[step_down, slot] = merged(step_down, slot, down_in[step_down, slot])
                down_copy(step_down).start()

        step_out = now - lag_out

        @pl.when(jnp.logical_and(step_out >= 0, step_out < steps))
        def _():
            rows = pl.ds(side * half + step_out * CHUNK, CHUNK)
            for slot in range(slots):
                passing = jnp.where(lower[slot], up_in[step_out, slot], down_in[step_out, slot])
                out_ref[slot, rows] = merged(step_out, slot, passing)
            out_copy(step_out, side).start()

    @pl.when(jnp.logical_not(has_below))
    def _():
        up_in[...] = jnp.zeros_like(up_in)

    @pl.when(jnp.logical_not(has_above))
    def _():
        down_in[...] = jnp.zeros_like(down_in)

    each(steps + line - 1, tick)

    def finish(step):
        beside_copy(step).wait_send()

        @pl.when(has_above)
        def _():
            up_copy(step).wait_send()

        @pl.when(has_below)
        def _():
            down_copy(step).wait_send()

        out_copy(step, side).wait_send()
        out_copy(step, 1 - side).wait_recv()

    each(steps, finish)


def spread(owners, blocks, line):
    slots = owners.shape[0]
    count, rows, width = blocks.shape
    steps = count // 2 // CHUNK
    store = pltpu.VMEM((steps, slots, CHUNK, rows, width), blocks.dtype)
    dma = pltpu.SemaphoreType.DMA((steps,))
    return pl.pallas_call(
        functools.partial(spread_kernel, line, slots),
        out_shape=jax.ShapeDtypeStruct((slots, count, rows, width), blocks.dtype),
        in_specs=[
            pl.BlockSpec(memory_space=pltpu.SMEM),
            pl.BlockSpec(memory_space=pltpu.VMEM),
        ],
        out_specs=pl.BlockSpec(memory_space=pltpu.VMEM),
        scratch_shapes=[
            pltpu.VMEM((steps, CHUNK, rows, width), blocks.dtype), store, store, store, store,
        ] + [dma] * 8,
        compiler_params=pltpu.CompilerParams(
            collective_id=0, has_side_effects=True, vmem_limit_bytes=VMEM_LIMIT
        ),
    )(owners, blocks)


def curve_kernel(slots, coef_ref, mine_ref, query_ref, out_ref, shifted, total):
    step = pl.program_id(0)
    channels, rows, width = mine_ref.shape[-3:]
    events = rows // PAIR

    @pl.when(step == 0)
    def _():
        total[...] = jnp.zeros_like(total)

    queries = jnp.concatenate(
        [
            jnp.concatenate(
                [query_ref[slot, side, 0, channel] for side in range(2) for slot in range(slots)],
                axis=0,
            )
            for channel in range(channels)
        ],
        axis=1,
    )
    columns = queries.shape[0]
    lane = lax.broadcasted_iota(jnp.int32, (events, columns), 1)
    second = (lane // events) % PAIR == 1
    later = lane >= columns // 2
    curves = []
    for side in range(2):
        for channel in range(channels):
            row = mine_ref[side, 0, channel].astype(jnp.float32)
            row = jnp.concatenate([row, jnp.zeros((rows, 128), jnp.float32)], axis=1)
            for index in range(LAGS):
                shift = (index - LAGS // 2) % (width + 128)
                moved = pltpu.roll(row, shift, axis=1) if shift else row
                shifted[side, pl.ds(index * rows, rows), pl.ds(channel * width, width)] = (
                    moved[:, :width].astype(jnp.bfloat16)
                )
        curves.append(
            lax.dot_general(
                shifted[side], queries, (((1,), (1,)), ((), ())),
                preferred_element_type=jnp.float32,
            ).reshape(LAGS, PAIR, events, columns)
        )
    picked = [jnp.where(second[None], each[:, 1], each[:, 0]) for each in curves]
    curve = jnp.where(later[None], picked[1], picked[0])
    for group in range(GROUPS):
        total[group] += curve * coef_ref[0, group][None, None, :]

    @pl.when(step == pl.num_programs(0) - 1)
    def _():
        quarter = LAGS // 4
        place = (lane // (columns // 2)) * 2 + (lane // events) % PAIR
        for group in range(GROUPS):
            values = total[group].reshape(LAGS * events, columns)
            values = values + pltpu.roll(values, columns // 2, axis=1)
            ahead = pltpu.roll(values, columns - events, axis=1)
            behind = pltpu.roll(values, events, axis=1)
            flag = (lax.broadcasted_iota(jnp.int32, values.shape, 1) // events) % PAIR == 1
            values = (values + jnp.where(flag, behind, ahead)).reshape(LAGS, events, columns)
            packed = values[:quarter]
            for part in range(1, 4):
                packed = jnp.where(
                    (place == part)[None], values[part * quarter : (part + 1) * quarter], packed
                )
            out_ref[group] = packed


def curves(coef, mine, queries):
    slots = queries.shape[0]
    channels, rows, width = mine.shape[-3:]
    steps = mine.shape[1]
    events = rows // PAIR
    columns = 2 * slots * rows
    return pl.pallas_call(
        functools.partial(curve_kernel, slots),
        grid=(steps,),
        out_shape=jax.ShapeDtypeStruct((GROUPS, LAGS // 4, events, columns), jnp.float32),
        in_specs=[
            pl.BlockSpec((1, GROUPS, columns), lambda i: (i, 0, 0)),
            pl.BlockSpec((2, 1, channels, rows, width), lambda i: (0, i, 0, 0, 0)),
            pl.BlockSpec((slots, 2, 1, channels, rows, width), lambda i: (0, 0, i, 0, 0, 0)),
        ],
        out_specs=pl.BlockSpec(
            (GROUPS, LAGS // 4, events, columns), lambda i: (0, 0, 0, 0)
        ),
        scratch_shapes=[
            pltpu.VMEM((2, LAGS * rows, channels * width), jnp.bfloat16),
            pltpu.VMEM((GROUPS, LAGS, events, columns), jnp.float32),
        ],
        compiler_params=pltpu.CompilerParams(vmem_limit_bytes=VMEM_LIMIT),
    )(coef, mine, queries)


def peak_kernel(parts, part_ref, out_ref, landed, send, recv, back_send, back_recv):
    tile, sta = lax.axis_index("tile"), lax.axis_index("sta")
    share = GROUPS // parts
    barrier = pltpu.get_barrier_semaphore()
    for hop in range(1, parts):
        pl.semaphore_signal(
            barrier, inc=1, device_id=(tile, lax.rem(sta + hop, parts)), device_id_type=MESH
        )
    pl.semaphore_wait(barrier, parts - 1)
    copies = []
    for hop in range(1, parts):
        target = lax.rem(sta + hop, parts)
        copy = pltpu.make_async_remote_copy(
            src_ref=part_ref.at[pl.ds(target * share, share)], dst_ref=landed.at[hop - 1],
            send_sem=send.at[hop - 1], recv_sem=recv.at[hop - 1],
            device_id=(tile, target), device_id_type=MESH,
        )
        copy.start()
        copies.append(copy)
    total = part_ref[pl.ds(sta * share, share)]
    for hop in range(1, parts):
        copies[hop - 1].wait_recv()
        total = total + landed[hop - 1]
    highest = jnp.max(total, axis=1)
    rows, columns = highest.shape[1:]
    highest = highest.reshape(share * rows, columns)
    highest = jnp.maximum(highest, pltpu.roll(highest, columns // 2, axis=1))
    flag = (lax.broadcasted_iota(jnp.int32, highest.shape, 1) // rows) % PAIR == 1
    highest = jnp.maximum(
        highest,
        jnp.where(
            flag, pltpu.roll(highest, rows, axis=1), pltpu.roll(highest, columns - rows, axis=1)
        ),
    )
    out_ref[pl.ds(sta * share, share)] = highest.reshape(share, rows, columns)
    backs = []
    for hop in range(1, parts):
        mine = pl.ds(sta * share, share)
        copy = pltpu.make_async_remote_copy(
            src_ref=out_ref.at[mine], dst_ref=out_ref.at[mine],
            send_sem=back_send.at[hop - 1], recv_sem=back_recv.at[hop - 1],
            device_id=(tile, lax.rem(sta + hop, parts)), device_id_type=MESH,
        )
        copy.start()
        backs.append(copy)
    for copy in copies:
        copy.wait_send()
    for hop in range(1, parts):
        backs[hop - 1].wait_send()
        theirs = pl.ds(lax.rem(sta + parts - hop, parts) * share, share)
        pltpu.make_async_remote_copy(
            src_ref=out_ref.at[theirs], dst_ref=out_ref.at[theirs],
            send_sem=back_send.at[hop - 1], recv_sem=back_recv.at[hop - 1],
            device_id=(tile, lax.rem(sta + hop, parts)), device_id_type=MESH,
        ).wait_recv()


def peaks(part, parts):
    groups, quarter, events, columns = part.shape
    share = groups // parts
    dma = pltpu.SemaphoreType.DMA((parts - 1,))
    return pl.pallas_call(
        functools.partial(peak_kernel, parts),
        out_shape=jax.ShapeDtypeStruct((groups, events, columns), jnp.float32),
        in_specs=[pl.BlockSpec(memory_space=pltpu.VMEM)],
        out_specs=pl.BlockSpec(memory_space=pltpu.VMEM),
        scratch_shapes=[
            pltpu.VMEM((parts - 1, share, quarter, events, columns), jnp.float32),
            dma, dma, dma, dma,
        ],
        compiler_params=pltpu.CompilerParams(
            collective_id=1, has_side_effects=True, vmem_limit_bytes=VMEM_LIMIT
        ),
    )(part)


def shards(tiles, parts, waves, valid, station_group, owners):
    stations, events, channels, samples = waves.shape
    slots = owners.shape[0]
    flags = jnp.concatenate([valid, station_group[:, None]], axis=1)
    everyone = lax.all_gather(flags, ("tile", "sta")).reshape(tiles, parts * stations, events + 1)

    pairs = stations // PAIR
    normed = normalize(waves, valid).reshape(pairs, PAIR, events, channels, samples)
    normed = normed.transpose(0, 3, 1, 2, 4).reshape(pairs * channels, PAIR * events, samples)
    queries = spread(owners, normed, tiles // 2)

    steps = pairs // 2
    shape = (2, steps, channels, PAIR * events, samples)
    onehot = (station_group[:, None] == jnp.arange(GROUPS, dtype=jnp.int32)[None, :]).astype(
        jnp.float32
    )
    coef = onehot.reshape(2, steps, PAIR, GROUPS).transpose(1, 3, 0, 2)
    coef = jnp.broadcast_to(
        coef[:, :, :, None, :, None], (steps, GROUPS, 2, slots, PAIR, events)
    ).reshape(steps, GROUPS, 2 * slots * PAIR * events)
    part = curves(coef, normed.reshape(shape), queries.reshape((slots,) + shape))
    highest = peaks(part, parts)
    highest = highest.reshape(GROUPS, events, 2, slots, PAIR, events)[:, :, 0, :, 0, :]
    highest = highest.reshape(GROUPS, events, slots * events).transpose(0, 2, 1)

    group_of = everyone[0, :, events]
    whole_onehot = (group_of[:, None] == jnp.arange(GROUPS, dtype=jnp.int32)[None, :]).astype(
        jnp.bfloat16
    )
    flags_of = everyone[:, :, :events].astype(jnp.bfloat16)
    query_valid = jnp.take(flags_of, owners, axis=0).transpose(1, 0, 2).reshape(-1, slots * events)
    local_valid = flags_of[lax.axis_index("tile")]
    common = jnp.einsum(
        "gsq,se->gqe", whole_onehot.T[:, :, None] * query_valid[None], local_valid,
        preferred_element_type=jnp.float32,
    )
    return highest / (samples * jnp.maximum(common, 1.0))


def solution(mesh):
    return jax.shard_map(
        functools.partial(shards, mesh.shape["tile"], mesh.shape["sta"]),
        mesh=mesh,
        in_specs=(P("sta", "tile", None, None), P("sta", "tile"), P("sta"), P()),
        out_specs=P(None, None, "tile"),
        check_vma=False,
    )
```

time: 398 us -> 157 us (0.39)
  waiting for transfers between devices: 171 us -> 0 us
  Pallas kernels: 0 us -> 110 us
  local copies, waits for them, and re-layouts: 105 us -> 6.34 us
  matrix products: 28.7 us -> 0.83 us
  other arithmetic: 29 us -> 1.39 us
  between operations: 16 us -> 0.18 us
  blocking collectives: 45.8 us -> 37.5 us
    psum x2 -> x0, waiting for transfers between devices: 171 us -> none  [the longest x1 132 us: from_root(): return lax.psum(jnp.where(mine, array, jnp.zeros_like(array)), axis)]
    pallas_call x0 -> x3, Pallas kernels: none -> 110 us  [the longest x1 72.6 us: spread(): pl.pallas_call(functools.partial(spread_kernel, line, slots), out_shape=j...]
    psum x2 -> x0, blocking collectives: 45.8 us -> none  [the longest x1 35.1 us: from_root(): return lax.psum(jnp.where(mine, array, jnp.zeros_like(array)), axis)]
    reshape x17 -> x4, local copies, waits for them, and re-layouts: 44.9 us -> 3.93 us  [the longest x1 1.56 us: shards(): highest.reshape(GROUPS, events, 2, slots, PAIR, events)[:, :, 0, :, 0, :]]
    all_gather x0 -> x1, blocking collectives: none -> 37.5 us  [shards(): lax.all_gather(flags, ('tile', 'sta'))]
    while x153 -> x0, local copies, waits for them, and re-layouts: 28.9 us -> none
    dot_general x17 -> x1, matrix products: 28.7 us -> 0.83 us  [shards(): jnp.einsum('gsq,se->gqe', whole_onehot.T[:, :, None] * query_valid[None],...]
    another operation x9 -> x1, other arithmetic: 18.4 us -> 0.01 us  [the longest x8 18.4 us: shifted_query(): jnp.stack([padded[:, :, :, SUB * offset:SUB * offset + length] for offset...]
  transfers between devices with their start and end apart: 2 -> 0, of which waited for: 2 -> 0; matrix products, arithmetic and copies ran while one was open for 0% -> 0% of each run, Pallas kernels for 0% -> 0%
where the time goes in v1:
time: 157 us
  Pallas kernels  110 us (70%)
  blocking collectives  37.5 us (24%)
  local copies, waits for them, and re-layouts  6.34 us (4%)
    pallas_call x1, Pallas kernels, spread(): pl.pallas_call(functools.partial(spread_kernel, line, slots), out_shape=j...  72.6 us
    all_gather x1, blocking collectives, shards(): lax.all_gather(flags, ('tile', 'sta'))  37.5 us
    pallas_call x1, Pallas kernels, curves(): pl.pallas_call(functools.partial(curve_kernel, slots), grid=(steps,), out...  25 us
    pallas_call x1, Pallas kernels, peaks(): pl.pallas_call(functools.partial(peak_kernel, parts), out_shape=jax.Shape...  12.8 us

profile of v1, /device:TPU:0, one launch (start us, length us, event | category | flops | bytes accessed | tf_op | source)
XLA Modules:
  0.0 156.7 jit_solution(1778671665093764962)
XLA Ops:
  0.0 0.8 eq.39
  0.9 0.2 broadcast_in_dim.16
  1.1 1.3 reshape.67.coef_ref
  2.4 0.7 convert_element_type.26
  3.1 0.1 copy.31
  3.2 0.0 copy-done
  3.2 0.2 fusion
  3.4 0.1 copy.29
  3.5 0.1 copy.30
  3.6 0.3 fusion.2
  3.9 1.0 copy.32
  4.9 72.6 %shard_map.46 = bf16[4,48,16,512]{3,2,1,0:T(8,128)(2,1)} custom-call(s32[4]{0:T(128)} %owners_ref.1, bf16[48,16,512]{2,1,0:T(8,128)(2,1)} %bitcast.25), custom_call_target="tpu_custom_call" | custom-call | tf_op jit(solution)/shard_map/pallas_call | solution.py:180
  77.5 0.0 copy-start.1
  77.5 0.0 copy-start.2
  77.5 25.0 %shard_map.47.part_ref = f32[8,16,8,128]{3,2,1,0:T(8,128)} custom-call(f32[8,8,128]{2,1,0:T(8,128)} %reshape.67.coef_ref, bf16[2,8,3,16,512]{4,3,2,1,0:T(8,128)(2,1)} %bitcast.26, bf16[4,2,8,3,16,512]{5,4,3,2,1,0:T(8,128)(2,1)} %bitcast.24), custom_call_target="tpu_custom_call" | custom-call | tf_op jit(solution)/shard_map/pallas_call | solution.py:267
  102.5 12.8 %shard_map.48 = f32[8,8,128]{2,1,0:T(8,128)} custom-call(f32[8,16,8,128]{3,2,1,0:T(8,128)} %shard_map.47.part_ref), custom_call_target="tpu_custom_call" | custom-call | tf_op jit(solution)/shard_map/pallas_call | solution.py:348
  115.3 1.6 reshape.71
  116.9 0.4 slice_reduce_fusion
  117.2 0.1 reshape_squeeze.3
  117.4 37.5 %all-gather.1 = s32[32,32,9]{1,2,0:T(8,128)S(1)} all-gather(s32[1,32,9]{1,2,0:T(8,128)S(1)} %add_bitcast_fusion), channel_id=2, replica_groups=mesh['tile'=8,'sta'=4] {'tile','sta'}, dimensions={0}, use_global_device_ids=true | all-gather | bytes 38016 | tf_op jit(solution)/shard_map/all_gather | solution.py:367
  155.0 0.1 reshape.72
  155.1 0.6 gather_fusion
  155.7 0.1 select_bitcast_fusion
  155.8 0.8 fusion.4
  (18 shorter events, 0.2 us)
Async XLA Ops:
  0.0 3.2 %copy-start = (bf16[32,8,3,512]{3,1,2,0:T(8,128)(2,1)S(1)}, bf16[32,8,3,512]{3,1,2,0:T(8,128)(2,1)}, u32[]{:S(2)}) copy-start(bf16[32,8,3,512]{3,1,2,0:T(8,128)(2,1)} %param.4) | copy-start | bytes 2359300
  77.5 39.9 %copy-start.1 = (s32[32,8]{0,1:T(8,128)S(1)}, s32[32,8]{0,1:T(8,128)}, u32[]{:S(2)}) copy-start(s32[32,8]{0,1:T(8,128)} %param.5) | copy-start | bytes 3076
  77.5 39.9 %copy-start.2 = (s32[32]{0:T(128)S(1)}, s32[32]{0:T(128)}, u32[]{:S(2)}) copy-start(s32[32]{0:T(128)} %param.6) | copy-start | bytes 388
  102.5 52.6 %copy-start.3 = (s32[4]{0:T(128)S(1)}, s32[4]{0:T(128)}, u32[]{:S(2)}) copy-start(s32[4]{0:T(128)} %owners_ref.1) | copy-start | bytes 52

commit v2 on v1

--- a/solution.py
+++ b/solution.py
@@ -25,9 +25,10 @@
 
 
 def spread_kernel(
-    line, slots, owners_ref, mine_ref, out_ref,
+    line, slots, owners_ref, mine_ref, flags_ref, out_ref, everyone_ref,
     beside, up_out, up_in, down_out, down_in,
     beside_send, beside_recv, up_send, up_recv, down_send, down_recv, out_send, out_recv,
+    flags_send, flags_recv, flags_local,
 ):
     tile, sta = lax.axis_index("tile"), lax.axis_index("sta")
     layer, side = tile // 2, tile % 2
@@ -37,20 +38,30 @@
     above, below = layer * 2 + 2 + side, layer * 2 - 2 + side
     has_above, has_below = layer < line - 1, layer > 0
 
+    tiles = 2 * line
+
+    def each(count, body):
+        def run(index, carry):
+            body(index)
+            return carry
+
+        lax.fori_loop(0, count, run, 0)
+
     barrier = pltpu.get_barrier_semaphore()
-    pl.semaphore_signal(barrier, inc=1, device_id=(other, sta), device_id_type=MESH)
-
-    @pl.when(has_above)
-    def _():
-        pl.semaphore_signal(barrier, inc=1, device_id=(above, sta), device_id_type=MESH)
-
-    @pl.when(has_below)
-    def _():
-        pl.semaphore_signal(barrier, inc=1, device_id=(below, sta), device_id_type=MESH)
-
-    pl.semaphore_wait(
-        barrier, 1 + has_above.astype(jnp.int32) + has_below.astype(jnp.int32)
-    )
+    each(
+        tiles - 1,
+        lambda hop: pl.semaphore_signal(
+            barrier, inc=1, device_id=(lax.rem(tile + 1 + hop, tiles), sta), device_id_type=MESH
+        ),
+    )
+    pl.semaphore_wait(barrier, tiles - 1)
+
+    def flags_copy(hop, row):
+        return pltpu.make_async_remote_copy(
+            src_ref=flags_ref, dst_ref=everyone_ref.at[row],
+            send_sem=flags_send.at[hop], recv_sem=flags_recv.at[hop],
+            device_id=(lax.rem(tile + 1 + hop, tiles), sta), device_id_type=MESH,
+        )
 
     def beside_copy(step):
         return pltpu.make_async_remote_copy(
@@ -82,14 +93,10 @@
             device_id=(other, sta), device_id_type=MESH,
         )
 
-    def each(count, body):
-        def run(index, carry):
-            body(index)
-            return carry
-
-        lax.fori_loop(0, count, run, 0)
-
     each(steps, lambda step: beside_copy(step).start())
+    each(tiles - 1, lambda hop: flags_copy(hop, tile).start())
+    own_flags = pltpu.make_async_copy(flags_ref, everyone_ref.at[tile], flags_local)
+    own_flags.start()
     own = [owners_ref[slot] == tile for slot in range(slots)]
     near = [owners_ref[slot] == other for slot in range(slots)]
     lower = [owners_ref[slot] < layer * 2 for slot in range(slots)]
@@ -169,9 +176,16 @@
         out_copy(step, 1 - side).wait_recv()
 
     each(steps, finish)
-
-
-def spread(owners, blocks, line):
+    own_flags.wait()
+
+    def finish_flags(hop):
+        flags_copy(hop, tile).wait_send()
+        flags_copy(hop, lax.rem(tile + tiles - 1 - hop, tiles)).wait_recv()
+
+    each(tiles - 1, finish_flags)
+
+
+def spread(owners, blocks, flags, line):
     slots = owners.shape[0]
     count, rows, width = blocks.shape
     steps = count // 2 // CHUNK
@@ -179,22 +193,35 @@
     dma = pltpu.SemaphoreType.DMA((steps,))
     return pl.pallas_call(
         functools.partial(spread_kernel, line, slots),
-        out_shape=jax.ShapeDtypeStruct((slots, count, rows, width), blocks.dtype),
+        out_shape=(
+            jax.ShapeDtypeStruct((slots, count, rows, width), blocks.dtype),
+            jax.ShapeDtypeStruct((2 * line,) + flags.shape, flags.dtype),
+        ),
         in_specs=[
             pl.BlockSpec(memory_space=pltpu.SMEM),
             pl.BlockSpec(memory_space=pltpu.VMEM),
-        ],
-        out_specs=pl.BlockSpec(memory_space=pltpu.VMEM),
+            pl.BlockSpec(memory_space=pltpu.VMEM),
+        ],
+        out_specs=(
+            pl.BlockSpec(memory_space=pltpu.VMEM),
+            pl.BlockSpec(memory_space=pltpu.VMEM),
+        ),
         scratch_shapes=[
             pltpu.VMEM((steps, CHUNK, rows, width), blocks.dtype), store, store, store, store,
-        ] + [dma] * 8,
+        ] + [dma] * 8 + [
+            pltpu.SemaphoreType.DMA((2 * line - 1,)), pltpu.SemaphoreType.DMA((2 * line - 1,)),
+            pltpu.SemaphoreType.DMA,
+        ],
         compiler_params=pltpu.CompilerParams(
             collective_id=0, has_side_effects=True, vmem_limit_bytes=VMEM_LIMIT
         ),
-    )(owners, blocks)
-
-
-def curve_kernel(slots, coef_ref, mine_ref, query_ref, out_ref, shifted, total):
+    )(owners, blocks, flags)
+
+
+def curve_kernel(
+    slots, owners_ref, coef_ref, member_ref, everyone_ref, mine_ref, query_ref,
+    out_ref, common_ref, shifted, total,
+):
     step = pl.program_id(0)
     channels, rows, width = mine_ref.shape[-3:]
     events = rows // PAIR
@@ -256,9 +283,14 @@
                     (place == part)[None], values[part * quarter : (part + 1) * quarter], packed
                 )
             out_ref[group] = packed
-
-
-def curves(coef, mine, queries):
+        flags = [everyone_ref[owners_ref[slot]] for slot in range(slots)]
+        flags = jnp.concatenate([each for each in flags for _ in range(PAIR)] * 2, axis=0)
+        common_ref[...] = lax.dot_general(
+            member_ref[...], flags, (((1,), (1,)), ((), ())), preferred_element_type=jnp.float32
+        ).reshape(common_ref.shape)
+
+
+def curves(owners, coef, member, everyone, mine, queries):
     slots = queries.shape[0]
     channels, rows, width = mine.shape[-3:]
     steps = mine.shape[1]
@@ -267,24 +299,34 @@
     return pl.pallas_call(
         functools.partial(curve_kernel, slots),
         grid=(steps,),
-        out_shape=jax.ShapeDtypeStruct((GROUPS, LAGS // 4, events, columns), jnp.float32),
+        out_shape=(
+            jax.ShapeDtypeStruct((GROUPS, LAGS // 4, events, columns), jnp.float32),
+            jax.ShapeDtypeStruct((GROUPS, events, columns), jnp.float32),
+        ),
         in_specs=[
+            pl.BlockSpec(memory_space=pltpu.SMEM),
             pl.BlockSpec((1, GROUPS, columns), lambda i: (i, 0, 0)),
+            pl.BlockSpec(memory_space=pltpu.VMEM),
+            pl.BlockSpec(memory_space=pltpu.VMEM),
             pl.BlockSpec((2, 1, channels, rows, width), lambda i: (0, i, 0, 0, 0)),
             pl.BlockSpec((slots, 2, 1, channels, rows, width), lambda i: (0, 0, i, 0, 0, 0)),
         ],
-        out_specs=pl.BlockSpec(
-            (GROUPS, LAGS // 4, events, columns), lambda i: (0, 0, 0, 0)
+        out_specs=(
+            pl.BlockSpec((GROUPS, LAGS // 4, events, columns), lambda i: (0, 0, 0, 0)),
+            pl.BlockSpec((GROUPS, events, columns), lambda i: (0, 0, 0)),
         ),
         scratch_shapes=[
             pltpu.VMEM((2, LAGS * rows, channels * width), jnp.bfloat16),
             pltpu.VMEM((GROUPS, LAGS, events, columns), jnp.float32),
         ],
         compiler_params=pltpu.CompilerParams(vmem_limit_bytes=VMEM_LIMIT),
-    )(coef, mine, queries)
-
-
-def peak_kernel(parts, part_ref, out_ref, landed, send, recv, back_send, back_recv):
+    )(owners, coef, member, everyone, mine, queries)
+
+
+def peak_kernel(
+    parts, samples, part_ref, common_ref, out_ref, landed, counted,
+    send, recv, count_send, count_recv, back_send, back_recv,
+):
     tile, sta = lax.axis_index("tile"), lax.axis_index("sta")
     share = GROUPS // parts
     barrier = pltpu.get_barrier_semaphore()
@@ -303,10 +345,24 @@
         )
         copy.start()
         copies.append(copy)
+    counts = []
+    for hop in range(1, parts):
+        target = lax.rem(sta + hop, parts)
+        copy = pltpu.make_async_remote_copy(
+            src_ref=common_ref.at[pl.ds(target * share, share)], dst_ref=counted.at[hop - 1],
+            send_sem=count_send.at[hop - 1], recv_sem=count_recv.at[hop - 1],
+            device_id=(tile, target), device_id_type=MESH,
+        )
+        copy.start()
+        counts.append(copy)
+    common = common_ref[pl.ds(sta * share, share)]
     total = part_ref[pl.ds(sta * share, share)]
     for hop in range(1, parts):
         copies[hop - 1].wait_recv()
         total = total + landed[hop - 1]
+    for hop in range(1, parts):
+        counts[hop - 1].wait_recv()
+        common = common + counted[hop - 1]
     highest = jnp.max(total, axis=1)
     rows, columns = highest.shape[1:]
     highest = highest.reshape(share * rows, columns)
@@ -318,7 +374,9 @@
             flag, pltpu.roll(highest, rows, axis=1), pltpu.roll(highest, columns - rows, axis=1)
         ),
     )
-    out_ref[pl.ds(sta * share, share)] = highest.reshape(share, rows, columns)
+    out_ref[pl.ds(sta * share, share)] = highest.reshape(share, rows, columns) / (
+        samples * jnp.maximum(common, 1.0)
+    )
     backs = []
     for hop in range(1, parts):
         mine = pl.ds(sta * share, share)
@@ -329,7 +387,7 @@
         )
         copy.start()
         backs.append(copy)
-    for copy in copies:
+    for copy in copies + counts:
         copy.wait_send()
     for hop in range(1, parts):
         backs[hop - 1].wait_send()
@@ -341,35 +399,35 @@
         ).wait_recv()
 
 
-def peaks(part, parts):
+def peaks(part, common, samples, parts):
     groups, quarter, events, columns = part.shape
     share = groups // parts
     dma = pltpu.SemaphoreType.DMA((parts - 1,))
     return pl.pallas_call(
-        functools.partial(peak_kernel, parts),
+        functools.partial(peak_kernel, parts, float(samples)),
         out_shape=jax.ShapeDtypeStruct((groups, events, columns), jnp.float32),
-        in_specs=[pl.BlockSpec(memory_space=pltpu.VMEM)],
+        in_specs=[pl.BlockSpec(memory_space=pltpu.VMEM)] * 2,
         out_specs=pl.BlockSpec(memory_space=pltpu.VMEM),
         scratch_shapes=[
             pltpu.VMEM((parts - 1, share, quarter, events, columns), jnp.float32),
-            dma, dma, dma, dma,
+            pltpu.VMEM((parts - 1, share, events, columns), jnp.float32),
+            dma, dma, dma, dma, dma, dma,
         ],
         compiler_params=pltpu.CompilerParams(
             collective_id=1, has_side_effects=True, vmem_limit_bytes=VMEM_LIMIT
         ),
-    )(part)
+    )(part, common)
 
 
 def shards(tiles, parts, waves, valid, station_group, owners):
     stations, events, channels, samples = waves.shape
     slots = owners.shape[0]
-    flags = jnp.concatenate([valid, station_group[:, None]], axis=1)
-    everyone = lax.all_gather(flags, ("tile", "sta")).reshape(tiles, parts * stations, events + 1)
+    flags = jnp.pad(valid.T.astype(jnp.float32), ((0, 0), (0, -stations % 128)))
 
     pairs = stations // PAIR
     normed = normalize(waves, valid).reshape(pairs, PAIR, events, channels, samples)
     normed = normed.transpose(0, 3, 1, 2, 4).reshape(pairs * channels, PAIR * events, samples)
-    queries = spread(owners, normed, tiles // 2)
+    queries, everyone = spread(owners, normed, flags, tiles // 2)
 
     steps = pairs // 2
     shape = (2, steps, channels, PAIR * events, samples)
@@ -380,23 +438,14 @@
     coef = jnp.broadcast_to(
         coef[:, :, :, None, :, None], (steps, GROUPS, 2, slots, PAIR, events)
     ).reshape(steps, GROUPS, 2 * slots * PAIR * events)
-    part = curves(coef, normed.reshape(shape), queries.reshape((slots,) + shape))
-    highest = peaks(part, parts)
+    members = jnp.pad(onehot.T, ((0, 0), (0, -stations % 128)))
+    member = (members[:, None, :] * flags[None]).reshape(GROUPS * events, -1)
+    part, common = curves(
+        owners, coef, member, everyone, normed.reshape(shape), queries.reshape((slots,) + shape)
+    )
+    highest = peaks(part, common, samples, parts)
     highest = highest.reshape(GROUPS, events, 2, slots, PAIR, events)[:, :, 0, :, 0, :]
-    highest = highest.reshape(GROUPS, events, slots * events).transpose(0, 2, 1)
-
-    group_of = everyone[0, :, events]
-    whole_onehot = (group_of[:, None] == jnp.arange(GROUPS, dtype=jnp.int32)[None, :]).astype(
-        jnp.bfloat16
-    )
-    flags_of = everyone[:, :, :events].astype(jnp.bfloat16)
-    query_valid = jnp.take(flags_of, owners, axis=0).transpose(1, 0, 2).reshape(-1, slots * events)
-    local_valid = flags_of[lax.axis_index("tile")]
-    common = jnp.einsum(
-        "gsq,se->gqe", whole_onehot.T[:, :, None] * query_valid[None], local_valid,
-        preferred_element_type=jnp.float32,
-    )
-    return highest / (samples * jnp.maximum(common, 1.0))
+    return highest.reshape(GROUPS, events, slots * events).transpose(0, 2, 1)
 
 
 def solution(mesh):

time: 157 us -> 125 us (0.80)
  blocking collectives: 37.5 us -> 0 us
  Pallas kernels: 110 us -> 115 us
  other arithmetic: 1.39 us -> 3.75 us
    all_gather x1 -> x0, blocking collectives: 37.5 us -> none  [shards(): lax.all_gather(flags, ('tile', 'sta'))]
    pallas_call x2, Pallas kernels: 85.4 us -> 89.5 us  [the longest x1 75.6 us: spread(): pl.pallas_call(functools.partial(spread_kernel, line, slots), out_shape=(...]
where the time goes in v2:
time: 125 us
  Pallas kernels  115 us (92%)
  local copies, waits for them, and re-layouts  6.16 us (5%)
  other arithmetic  3.75 us (3%)
    pallas_call x1, Pallas kernels, spread(): pl.pallas_call(functools.partial(spread_kernel, line, slots), out_shape=(...  75.6 us
    pallas_call x1, Pallas kernels, curves(): pl.pallas_call(functools.partial(curve_kernel, slots), grid=(steps,), out...  25.1 us
    pallas_call x1, Pallas kernels, peaks(): pl.pallas_call(functools.partial(peak_kernel, parts, float(samples)), out...  14 us

profile of v2, /device:TPU:0, one launch (start us, length us, event | category | flops | bytes accessed | tf_op | source)
XLA Modules:
  0.0 124.6 jit_solution(17567092975855258791)
XLA Ops:
  0.0 0.0 copy-start
  0.0 0.7 iota_compare_fusion
  0.7 0.7 eq.26
  1.5 0.7 fusion.3
  2.2 0.0 copy-start.1
  2.2 0.1 copy.18
  2.3 0.6 multiply_bitcast_fusion.member_ref
  2.9 1.4 %fusion = f32[32,8,3]{1,2,0:T(4,128)S(1)} fusion(bf16[32,8,3,512]{3,1,2,0:T(8,128)(2,1)} %param.4), kind=kLoop, calls=%fused_computation.2 | loop fusion | flops 1178880 | bytes 789504 | tf_op jit(solution)/shard_map/reduce_sum | solution.py:21
  4.3 0.1 copy.16
  4.4 0.1 copy.17
  4.5 0.2 broadcast_in_dim.2
  4.7 1.3 %reshape.42.coef_ref = f32[8,8,128]{2,1,0:T(8,128)} reshape(f32[8,8,2,4,2,8]{5,4,3,2,1,0:T(2,128)S(1)} %broadcast_in_dim.2) | data formatting | bytes 65536 | tf_op jit(solution)/shard_map/reshape | solution.py:440
  6.0 0.0 copy-done
  6.0 0.3 fusion.2
  6.3 0.0 copy-done.1
  6.3 1.0 copy.19
  7.3 75.6 %shard_map.46 = (bf16[4,48,16,512]{3,2,1,0:T(8,128)(2,1)}, f32[8,8,128]{2,1,0:T(8,128)}) custom-call(s32[4]{0:T(128)} %owners_ref.3, bf16[48,16,512]{2,1,0:T(8,128)(2,1)} %bitcast.13, f32[8,128]{1,0:T(8,128)} %copy-done.1), custom_call_target="tpu_custom_call" | custom-call | tf_op jit(solution)/shard_map/pallas_call | solution.py:194
  82.9 25.1 %shard_map.47 = (f32[8,16,8,128]{3,2,1,0:T(8,128)}, f32[8,8,128]{2,1,0:T(8,128)}) custom-call(s32[4]{0:T(128)} %owners_ref.3, f32[8,8,128]{2,1,0:T(8,128)} %reshape.42.coef_ref, f32[64,128]{1,0:T(8,128)} %multiply_bitcast_fusion.member_ref, f32[8,8,128]{2,1,0:T(8,128)} %get-tuple-element.9.everyone_ref, bf16[2,8,3,16,512]{4,3,2,1,0:T(8,128)(2,1)} %bitcast.14, ...), custom_call_target="tpu_custom_call" | custom-call | tf_op jit(solution)/shard_map/pallas_call | solution.py:299
  108.0 14.0 %shard_map.48 = f32[8,8,128]{2,1,0:T(8,128)} custom-call(f32[8,16,8,128]{3,2,1,0:T(8,128)} %get-tuple-element.11.part_ref, f32[8,8,128]{2,1,0:T(8,128)} %get-tuple-element.12.common_ref), custom_call_target="tpu_custom_call" | custom-call | tf_op jit(solution)/shard_map/pallas_call | solution.py:406
  122.0 1.6 %reshape.46 = f32[8,8,2,4,2,8]{5,4,3,2,1,0:T(2,128)S(1)} reshape(f32[8,8,128]{2,1,0:T(8,128)} %shard_map.48) | data formatting | bytes 65536 | tf_op jit(solution)/shard_map/reshape | solution.py:447
  123.5 0.4 slice_reduce_fusion
  123.9 0.7 reshape_squeeze.3
  (5 shorter events, 0.1 us)
Async XLA Ops:
  0.0 6.0 %copy-start = (bf16[32,8,3,512]{3,1,2,0:T(8,128)(2,1)S(1)}, bf16[32,8,3,512]{3,1,2,0:T(8,128)(2,1)}, u32[]{:S(2)}) copy-start(bf16[32,8,3,512]{3,1,2,0:T(8,128)(2,1)} %param.4) | copy-start | bytes 2359300
  2.2 4.1 %copy-start.1 = (f32[8,128]{1,0:T(8,128)}, f32[8,128]{1,0:T(8,128)S(1)}, u32[]{:S(2)}) copy-start(f32[8,128]{1,0:T(8,128)S(1)} %pad.12.flags_ref) | copy-start | bytes 12292

commit v3 on v2

v3 whole, which is shorter than its diff:
```python
import functools

import jax
import jax.numpy as jnp
from jax import lax
from jax.experimental import pallas as pl
from jax.experimental.pallas import tpu as pltpu
from jax.sharding import PartitionSpec as P

LAGS = 64
GROUPS = 8
PAIR = 2
CHUNK = 1
HOP = 2
AHEAD = 4
epsilon = 1e-06
MESH = pl.DeviceIdType.MESH
VMEM_LIMIT = 56 * 1024 * 1024


def normalize(raw_block, mask_block):
    signal = raw_block.astype(jnp.float32)
    inverse_rms = lax.rsqrt(jnp.mean(signal * signal, axis=-1, keepdims=True) + epsilon)
    return (signal * inverse_rms * mask_block[:, :, None, None].astype(jnp.float32)).astype(
        jnp.bfloat16
    )


def peak_kernel(
    line, parts, slots, samples,
    owners_ref, mine_ref, flags_ref, coef_ref, member_ref, peak_ref,
    out_ref, everyone_ref, shifted, products, total, part, landed, common_ref, counted,
    beside, up_out, up_in, down_out, down_in,
    beside_send, beside_recv, up_send, up_recv, down_send, down_recv, out_send, out_recv,
    flags_send, flags_recv, flags_local,
    send, recv, count_send, count_recv, back_send, back_recv,
):
    tile, sta = lax.axis_index("tile"), lax.axis_index("sta")
    layer, side = tile // 2, tile % 2
    other = layer * 2 + (1 - side)
    half = mine_ref.shape[0] // 2
    steps = half // CHUNK
    above, below = layer * 2 + 2 + side, layer * 2 - 2 + side
    has_above, has_below = layer < line - 1, layer > 0

    tiles = 2 * line

    def each(count, body):
        def run(index, carry):
            body(index)
            return carry

        lax.fori_loop(0, count, run, 0)

    barrier = pltpu.get_barrier_semaphore()
    each(
        tiles - 1,
        lambda hop: pl.semaphore_signal(
            barrier, inc=1, device_id=(lax.rem(tile + 1 + hop, tiles), sta), device_id_type=MESH
        ),
    )
    for hop in range(1, parts):
        pl.semaphore_signal(
            barrier, inc=1, device_id=(tile, lax.rem(sta + hop, parts)), device_id_type=MESH
        )
    pl.semaphore_wait(barrier, tiles - 1 + parts - 1)

    def flags_copy(hop, row):
        return pltpu.make_async_remote_copy(
            src_ref=flags_ref, dst_ref=everyone_ref.at[row],
            send_sem=flags_send.at[hop], recv_sem=flags_recv.at[hop],
            device_id=(lax.rem(tile + 1 + hop, tiles), sta), device_id_type=MESH,
        )

    def beside_copy(step):
        return pltpu.make_async_remote_copy(
            src_ref=mine_ref.at[pl.ds((1 - side) * half + step * CHUNK, CHUNK)],
            dst_ref=beside.at[step],
            send_sem=beside_send.at[step], recv_sem=beside_recv.at[step],
            device_id=(other, sta), device_id_type=MESH,
        )

    def up_copy(step):
        return pltpu.make_async_remote_copy(
            src_ref=up_out.at[step], dst_ref=up_in.at[step],
            send_sem=up_send.at[step], recv_sem=up_recv.at[step],
            device_id=(above, sta), device_id_type=MESH,
        )

    def down_copy(step):
        return pltpu.make_async_remote_copy(
            src_ref=down_out.at[step], dst_ref=down_in.at[step],
            send_sem=down_send.at[step], recv_sem=down_recv.at[step],
            device_id=(below, sta), device_id_type=MESH,
        )

    def out_copy(step, of_side):
        rows = pl.ds(of_side * half + step * CHUNK, CHUNK)
        return pltpu.make_async_remote_copy(
            src_ref=out_ref.at[:, rows], dst_ref=out_ref.at[:, rows],
            send_sem=out_send.at[step], recv_sem=out_recv.at[step],
            device_id=(other, sta), device_id_type=MESH,
        )

    each(AHEAD, lambda step: beside_copy(step).start())
    each(tiles - 1, lambda hop: flags_copy(hop, tile).start())
    own_flags = pltpu.make_async_copy(flags_ref, everyone_ref.at[tile], flags_local)
    own_flags.start()
    own = [owners_ref[slot] == tile for slot in range(slots)]
    near = [owners_ref[slot] == other for slot in range(slots)]
    lower = [owners_ref[slot] < layer * 2 for slot in range(slots)]

    def merged(step, slot, passing):
        local = mine_ref[pl.ds(side * half + step * CHUNK, CHUNK)]
        return jnp.where(own[slot], local, jnp.where(near[slot], beside[step], passing))

    rows, width = mine_ref.shape[-2:]
    events = rows // PAIR
    columns = 2 * slots * rows
    share = GROUPS // parts
    lane = lax.broadcasted_iota(jnp.int32, (events, columns), 1)
    second = (lane // events) % PAIR == 1
    later = lane >= columns // 2
    channels = mine_ref.shape[0] // (2 * coef_ref.shape[0])
    total[...] = jnp.zeros_like(total)

    def correlate(step):
        channel, quad = lax.rem(step, channels), step // channels
        queries = jnp.concatenate(
            [out_ref[slot, of_side * half + step] for of_side in range(2) for slot in range(slots)],
            axis=0,
        )
        for of_side in range(2):
            row = mine_ref[of_side * half + step].astype(jnp.float32)
            row = jnp.concatenate([row, jnp.zeros((rows, 128), jnp.float32)], axis=1)
            for index in range(LAGS):
                shift = (index - LAGS // 2) % (width + 128)
                moved = pltpu.roll(row, shift, axis=1) if shift else row
                shifted[of_side, pl.ds(index * rows, rows)] = moved[:, :width].astype(jnp.bfloat16)
            product = lax.dot_general(
                shifted[of_side], queries, (((1,), (1,)), ((), ())),
                preferred_element_type=jnp.float32,
            )

            @pl.when(channel == 0)
            def _():
                products[of_side] = product

            @pl.when(channel > 0)
            def _():
                products[of_side] += product

        @pl.when(channel == channels - 1)
        def _():
            def gather(index, carry):
                both = [
                    products[of_side, pl.ds(pl.multiple_of(index * rows, rows), rows)]
                    for of_side in range(2)
                ]
                picked = [jnp.where(second, one[events:], one[:events]) for one in both]
                curve = jnp.where(later, picked[1], picked[0])
                for group in range(GROUPS):
                    total[group, index] += curve * coef_ref[quad, pl.ds(group, 1)]
                return carry

            lax.fori_loop(0, LAGS, gather, 0, unroll=4)

    lag_up, lag_down = HOP * layer, HOP * (line - 1 - layer)
    lag_out = jnp.maximum(lag_up, lag_down)

    def tick(now):
        @pl.when(now < steps)
        def _():
            beside_copy(now).wait_recv()

        @pl.when(now + AHEAD < steps)
        def _():
            beside_copy(now + AHEAD).start()

        step_up = now - lag_up

        @pl.when(jnp.logical_and(step_up >= 0, step_up < steps))
        def _():
            @pl.when(has_below)
            def _():
                up_copy(step_up).wait_recv()

            @pl.when(has_above)
            def _():
                for slot in range(slots):
                    up_out[step_up, slot] = merged(step_up, slot, up_in[step_up, slot])
                up_copy(step_up).start()

        step_down = now - lag_down

        @pl.when(jnp.logical_and(step_down >= 0, step_down < steps))
        def _():
            @pl.when(has_above)
            def _():
                down_copy(step_down).wait_recv()

            @pl.when(has_below)
            def _():
                for slot in range(slots):
                    down_out[step_down, slot] = merged(step_down, slot, down_in[step_down, slot])
                down_copy(step_down).start()

        step_out = now - lag_out

        @pl.when(jnp.logical_and(step_out >= 0, step_out < steps))
        def _():
            rows = pl.ds(side * half + step_out * CHUNK, CHUNK)
            for slot in range(slots):
                passing = jnp.where(lower[slot], up_in[step_out, slot], down_in[step_out, slot])
                out_ref[slot, rows] = merged(step_out, slot, passing)
            out_copy(step_out, side).start()

        step_curve = step_out - HOP

        @pl.when(jnp.logical_and(step_curve >= 0, step_curve < steps))
        def _():
            out_copy(step_curve, 1 - side).wait_recv()
            correlate(step_curve)

    @pl.when(jnp.logical_not(has_below))
    def _():
        up_in[...] = jnp.zeros_like(up_in)

    @pl.when(jnp.logical_not(has_above))
    def _():
        down_in[...] = jnp.zeros_like(down_in)

    each(steps + HOP * line, tick)

    def finish(step):
        beside_copy(step).wait_send()

        @pl.when(has_above)
        def _():
            up_copy(step).wait_send()

        @pl.when(has_below)
        def _():
            down_copy(step).wait_send()

        out_copy(step, side).wait_send()

    each(steps, finish)
    own_flags.wait()

    def finish_flags(hop):
        flags_copy(hop, tile).wait_send()
        flags_copy(hop, lax.rem(tile + tiles - 1 - hop, tiles)).wait_recv()

    each(tiles - 1, finish_flags)

    quarter = LAGS // 4
    place = (lane // (columns // 2)) * 2 + (lane // events) % PAIR
    flags = [everyone_ref[owners_ref[slot]] for slot in range(slots)]
    flags = jnp.concatenate([one for one in flags for _ in range(PAIR)] * 2, axis=0)
    common_ref[...] = lax.dot_general(
        member_ref[...], flags, (((1,), (1,)), ((), ())), preferred_element_type=jnp.float32
    ).reshape(common_ref.shape)

    def pack(group):
        values = total[group].reshape(LAGS * events, columns)
        values = values + pltpu.roll(values, columns // 2, axis=1)
        ahead = pltpu.roll(values, columns - events, axis=1)
        behind = pltpu.roll(values, events, axis=1)
        flag = (lax.broadcasted_iota(jnp.int32, values.shape, 1) // events) % PAIR == 1
        values = (values + jnp.where(flag, behind, ahead)).reshape(LAGS, events, columns)
        packed = values[:quarter]
        for number in range(1, 4):
            packed = jnp.where(
                (place == number)[None], values[number * quarter : (number + 1) * quarter], packed
            )
        part[group] = packed

    copies, counts = [], []
    for hop in range(1, parts + 1):
        target = lax.rem(sta + hop, parts)
        for number in range(share):
            pack(target * share + number)
        if hop == parts:
            break
        theirs = pl.ds(target * share, share)
        for source, place_in, done, came, started in (
            (part, landed, send, recv, copies),
            (common_ref, counted, count_send, count_recv, counts),
        ):
            copy = pltpu.make_async_remote_copy(
                src_ref=source.at[theirs], dst_ref=place_in.at[hop - 1],
                send_sem=done.at[hop - 1], recv_sem=came.at[hop - 1],
                device_id=(tile, target), device_id_type=MESH,
            )
            copy.start()
            started.append(copy)
    ours = pl.ds(sta * share, share)
    common, summed = common_ref[ours], part[ours]
    for hop in range(1, parts):
        copies[hop - 1].wait_recv()
        summed = summed + landed[hop - 1]
    for hop in range(1, parts):
        counts[hop - 1].wait_recv()
        common = common + counted[hop - 1]
    highest = jnp.max(summed, axis=1)
    highest = highest.reshape(share * events, columns)
    highest = jnp.maximum(highest, pltpu.roll(highest, columns // 2, axis=1))
    flag = (lax.broadcasted_iota(jnp.int32, highest.shape, 1) // events) % PAIR == 1
    highest = jnp.maximum(
        highest,
        jnp.where(
            flag, pltpu.roll(highest, events, axis=1), pltpu.roll(highest, columns - events, axis=1)
        ),
    )
    peak_ref[pl.ds(sta * share, share)] = highest.reshape(share, events, columns) / (
        samples * jnp.maximum(common, 1.0)
    )
    backs = []
    for hop in range(1, parts):
        mine = pl.ds(sta * share, share)
        copy = pltpu.make_async_remote_copy(
            src_ref=peak_ref.at[mine], dst_ref=peak_ref.at[mine],
            send_sem=back_send.at[hop - 1], recv_sem=back_recv.at[hop - 1],
            device_id=(tile, lax.rem(sta + hop, parts)), device_id_type=MESH,
        )
        copy.start()
        backs.append(copy)
    for copy in copies + counts:
        copy.wait_send()
    for hop in range(1, parts):
        backs[hop - 1].wait_send()
        theirs = pl.ds(lax.rem(sta + parts - hop, parts) * share, share)
        pltpu.make_async_remote_copy(
            src_ref=peak_ref.at[theirs], dst_ref=peak_ref.at[theirs],
            send_sem=back_send.at[hop - 1], recv_sem=back_recv.at[hop - 1],
            device_id=(tile, lax.rem(sta + hop, parts)), device_id_type=MESH,
        ).wait_recv()


def peaks(owners, blocks, flags, coef, member, line, parts, samples):
    slots = owners.shape[0]
    count, rows, width = blocks.shape
    events = rows // PAIR
    columns = 2 * slots * rows
    share = GROUPS // parts
    steps = count // 2 // CHUNK
    store = pltpu.VMEM((steps, slots, CHUNK, rows, width), blocks.dtype)
    dma = pltpu.SemaphoreType.DMA((steps,))
    dma_tile = pltpu.SemaphoreType.DMA((2 * line - 1,))
    dma_sta = pltpu.SemaphoreType.DMA((parts - 1,))
    return pl.pallas_call(
        functools.partial(peak_kernel, line, parts, slots, float(samples)),
        out_shape=jax.ShapeDtypeStruct((GROUPS, events, columns), jnp.float32),
        in_specs=[pl.BlockSpec(memory_space=pltpu.SMEM)]
        + [pl.BlockSpec(memory_space=pltpu.VMEM)] * 4,
        out_specs=pl.BlockSpec(memory_space=pltpu.VMEM),
        scratch_shapes=[
            pltpu.VMEM((slots, count, rows, width), blocks.dtype),
            pltpu.VMEM((2 * line,) + flags.shape, flags.dtype),
            pltpu.VMEM((2, LAGS * rows, width), blocks.dtype),
            pltpu.VMEM((2, LAGS * rows, columns), jnp.float32),
            pltpu.VMEM((GROUPS, LAGS, events, columns), jnp.float32),
            pltpu.VMEM((GROUPS, LAGS // 4, events, columns), jnp.float32),
            pltpu.VMEM((parts - 1, share, LAGS // 4, events, columns), jnp.float32),
            pltpu.VMEM((GROUPS, events, columns), jnp.float32),
            pltpu.VMEM((parts - 1, share, events, columns), jnp.float32),
            pltpu.VMEM((steps, CHUNK, rows, width), blocks.dtype), store, store, store, store,
        ]
        + [dma] * 8
        + [dma_tile, dma_tile, pltpu.SemaphoreType.DMA]
        + [dma_sta] * 6,
        compiler_params=pltpu.CompilerParams(
            collective_id=0, has_side_effects=True, vmem_limit_bytes=VMEM_LIMIT
        ),
    )(owners, blocks, flags, coef, member)


def shards(tiles, parts, waves, valid, station_group, owners):
    stations, events, channels, samples = waves.shape
    slots = owners.shape[0]
    flags = jnp.pad(valid.T.astype(jnp.float32), ((0, 0), (0, -stations % 128)))

    pairs = stations // PAIR
    normed = normalize(waves, valid).reshape(pairs, PAIR, events, channels, samples)
    normed = normed.transpose(0, 3, 1, 2, 4).reshape(pairs * channels, PAIR * events, samples)

    steps = pairs // 2
    onehot = (station_group[:, None] == jnp.arange(GROUPS, dtype=jnp.int32)[None, :]).astype(
        jnp.float32
    )
    coef = onehot.reshape(2, steps, PAIR, GROUPS).transpose(1, 3, 0, 2)
    coef = jnp.broadcast_to(
        coef[:, :, :, None, :, None], (steps, GROUPS, 2, slots, PAIR, events)
    ).reshape(steps, GROUPS, 2 * slots * PAIR * events)
    members = jnp.pad(onehot.T, ((0, 0), (0, -stations % 128)))
    member = (members[:, None, :] * flags[None]).reshape(GROUPS * events, -1)
    highest = peaks(owners, normed, flags, coef, member, tiles // 2, parts, samples)
    highest = highest.reshape(GROUPS, events, 2, slots, PAIR, events)[:, :, 0, :, 0, :]
    return highest.reshape(GROUPS, events, slots * events).transpose(0, 2, 1)


def solution(mesh):
    return jax.shard_map(
        functools.partial(shards, mesh.shape["tile"], mesh.shape["sta"]),
        mesh=mesh,
        in_specs=(P("sta", "tile", None, None), P("sta", "tile"), P("sta"), P()),
        out_specs=P(None, None, "tile"),
        check_vma=False,
    )
```

time: 125 us -> 90.3 us (0.72)
  Pallas kernels: 115 us -> 81.4 us
    pallas_call x3 -> x1, Pallas kernels: 115 us -> 81.4 us  [peaks(): pl.pallas_call(functools.partial(peak_kernel, line, parts, slots, float(s...]
where the time goes in v3:
time: 90.3 us; the launch traced here: 90.1 us
  Pallas kernels  81.4 us (90%)
  local copies, waits for them, and re-layouts  5.5 us (6%)
  other arithmetic  3.09 us (3%)
    pallas_call x1, Pallas kernels, peaks(): pl.pallas_call(functools.partial(peak_kernel, line, parts, slots, float(s...  81.4 us

profile of v3, /device:TPU:0, one launch (start us, length us, event | category | flops | bytes accessed | tf_op | source)
XLA Modules:
  0.0 90.1 jit_solution(14928681768131687722)
XLA Ops:
  0.0 0.0 copy-start
  0.0 0.8 convert_bitcast_fusion
  0.8 0.1 copy.17
  0.8 1.4 %fusion = f32[32,8,3]{1,2,0:T(4,128)S(1)} fusion(bf16[32,8,3,512]{3,1,2,0:T(8,128)(2,1)} %param.4), kind=kLoop, calls=%fused_computation.2 | loop fusion | flops 1178880 | bytes 789504 | tf_op jit(solution)/shard_map/reduce_sum | solution.py:23
  2.2 0.1 copy.15
  2.3 0.1 copy.16
  2.4 0.0 copy-done
  2.4 0.3 fusion.2
  2.7 0.0 copy-start.2
  2.7 1.0 %copy.18 = bf16[16,2,8,3,512]{4,2,1,3,0:T(8,128)(2,1)} copy(bf16[16,2,8,3,512]{4,2,3,1,0:T(8,128)(2,1)S(1)} %bitcast.11) | data formatting | bytes 1572864 | tf_op jit(solution)/shard_map/reshape | solution.py:385
  3.7 0.0 copy-done.2
  3.7 0.0 copy-start.1
  3.7 0.1 eq.26
  3.8 0.2 broadcast_in_dim.2
  4.1 1.3 %reshape.41.coef_ref = f32[8,8,128]{2,1,0:T(8,128)} reshape(f32[8,8,2,4,2,8]{5,4,3,2,1,0:T(2,128)S(1)} %broadcast_in_dim.2) | data formatting | bytes 65536 | tf_op jit(solution)/shard_map/reshape | solution.py:395
  5.4 0.6 multiply_bitcast_fusion.member_ref
  6.0 0.0 copy-done.1
  6.0 81.4 %shard_map.46 = f32[8,8,128]{2,1,0:T(8,128)} custom-call(s32[4]{0:T(128)} %owners_ref.1, bf16[48,16,512]{2,1,0:T(8,128)(2,1)} %bitcast.10, f32[8,128]{1,0:T(8,128)} %copy-done.1, f32[8,8,128]{2,1,0:T(8,128)} %reshape.41.coef_ref, f32[64,128]{1,0:T(8,128)} %multiply_bitcast_fusion.member_ref), custom_call_target="tpu_custom_call" | custom-call | tf_op jit(solution)/shard_map/pallas_call | solution.py:352
  87.4 1.6 %reshape.42 = f32[8,8,2,4,2,8]{5,4,3,2,1,0:T(2,128)S(1)} reshape(f32[8,8,128]{2,1,0:T(8,128)} %shard_map.46) | data formatting | bytes 65536 | tf_op jit(solution)/shard_map/reshape | solution.py:399
  89.0 0.4 slice_reduce_fusion
  89.4 0.7 reshape_squeeze.3
  (6 shorter events, 0.1 us)
Async XLA Ops:
  0.0 2.4 %copy-start = (bf16[32,8,3,512]{3,1,2,0:T(8,128)(2,1)S(1)}, bf16[32,8,3,512]{3,1,2,0:T(8,128)(2,1)}, u32[]{:S(2)}) copy-start(bf16[32,8,3,512]{3,1,2,0:T(8,128)(2,1)} %param.4) | copy-start | bytes 2359300
  2.7 1.0 %copy-start.2 = (s32[32]{0:T(128)S(1)}, s32[32]{0:T(128)}, u32[]{:S(2)}) copy-start(s32[32]{0:T(128)} %param.6) | copy-start | bytes 388
  3.7 2.3 %copy-start.1 = (f32[8,128]{1,0:T(8,128)}, f32[8,128]{1,0:T(8,128)S(1)}, u32[]{:S(2)}) copy-start(f32[8,128]{1,0:T(8,128)S(1)} %pad.10.flags_ref) | copy-start | bytes 12292

commit v4 on v3

--- a/solution.py
+++ b/solution.py
@@ -11,7 +11,7 @@
 GROUPS = 8
 PAIR = 2
 CHUNK = 1
-HOP = 2
+HOP = 3
 AHEAD = 4
 epsilon = 1e-06
 MESH = pl.DeviceIdType.MESH
@@ -28,7 +28,7 @@
 
 def peak_kernel(
     line, parts, slots, samples,
-    owners_ref, mine_ref, flags_ref, coef_ref, member_ref, peak_ref,
+    owners_ref, group_ref, mine_ref, flags_ref, member_ref, peak_ref,
     out_ref, everyone_ref, shifted, products, total, part, landed, common_ref, counted,
     beside, up_out, up_in, down_out, down_in,
     beside_send, beside_recv, up_send, up_recv, down_send, down_recv, out_send, out_recv,
@@ -121,7 +121,7 @@
     lane = lax.broadcasted_iota(jnp.int32, (events, columns), 1)
     second = (lane // events) % PAIR == 1
     later = lane >= columns // 2
-    channels = mine_ref.shape[0] // (2 * coef_ref.shape[0])
+    channels = 2 * half // (group_ref.shape[0] // PAIR)
     total[...] = jnp.zeros_like(total)
 
     def correlate(step):
@@ -152,6 +152,14 @@
 
         @pl.when(channel == channels - 1)
         def _():
+            ahead, behind = quad * PAIR, half // channels * PAIR + quad * PAIR
+            group_of = jnp.where(
+                later,
+                jnp.where(second, group_ref[behind + 1], group_ref[behind]),
+                jnp.where(second, group_ref[ahead + 1], group_ref[ahead]),
+            )
+            coef = [(group_of == group).astype(jnp.float32) for group in range(GROUPS)]
+
             def gather(index, carry):
                 both = [
                     products[of_side, pl.ds(pl.multiple_of(index * rows, rows), rows)]
@@ -160,7 +168,7 @@
                 picked = [jnp.where(second, one[events:], one[:events]) for one in both]
                 curve = jnp.where(later, picked[1], picked[0])
                 for group in range(GROUPS):
-                    total[group, index] += curve * coef_ref[quad, pl.ds(group, 1)]
+                    total[group, index] += curve * coef[group]
                 return carry
 
             lax.fori_loop(0, LAGS, gather, 0, unroll=4)
@@ -220,7 +228,7 @@
         @pl.when(jnp.logical_and(step_curve >= 0, step_curve < steps))
         def _():
             out_copy(step_curve, 1 - side).wait_recv()
-            correlate(step_curve)
+            each(CHUNK, lambda number: correlate(step_curve * CHUNK + number))
 
     @pl.when(jnp.logical_not(has_below))
     def _():
@@ -258,8 +266,11 @@
     place = (lane // (columns // 2)) * 2 + (lane // events) % PAIR
     flags = [everyone_ref[owners_ref[slot]] for slot in range(slots)]
     flags = jnp.concatenate([one for one in flags for _ in range(PAIR)] * 2, axis=0)
+    member = jnp.concatenate(
+        [jnp.where(member_ref[...] == group, flags_ref[...], 0.0) for group in range(GROUPS)], axis=0
+    )
     common_ref[...] = lax.dot_general(
-        member_ref[...], flags, (((1,), (1,)), ((), ())), preferred_element_type=jnp.float32
+        member, flags, (((1,), (1,)), ((), ())), preferred_element_type=jnp.float32
     ).reshape(common_ref.shape)
 
     def pack(group):
@@ -338,7 +349,7 @@
         ).wait_recv()
 
 
-def peaks(owners, blocks, flags, coef, member, line, parts, samples):
+def peaks(owners, station_group, blocks, flags, members, line, parts, samples):
     slots = owners.shape[0]
     count, rows, width = blocks.shape
     events = rows // PAIR
@@ -352,8 +363,8 @@
     return pl.pallas_call(
         functools.partial(peak_kernel, line, parts, slots, float(samples)),
         out_shape=jax.ShapeDtypeStruct((GROUPS, events, columns), jnp.float32),
-        in_specs=[pl.BlockSpec(memory_space=pltpu.SMEM)]
-        + [pl.BlockSpec(memory_space=pltpu.VMEM)] * 4,
+        in_specs=[pl.BlockSpec(memory_space=pltpu.SMEM)] * 2
+        + [pl.BlockSpec(memory_space=pltpu.VMEM)] * 3,
         out_specs=pl.BlockSpec(memory_space=pltpu.VMEM),
         scratch_shapes=[
             pltpu.VMEM((slots, count, rows, width), blocks.dtype),
@@ -373,7 +384,7 @@
         compiler_params=pltpu.CompilerParams(
             collective_id=0, has_side_effects=True, vmem_limit_bytes=VMEM_LIMIT
         ),
-    )(owners, blocks, flags, coef, member)
+    )(owners, station_group, blocks, flags, members)
 
 
 def shards(tiles, parts, waves, valid, station_group, owners):
@@ -385,17 +396,8 @@
     normed = normalize(waves, valid).reshape(pairs, PAIR, events, channels, samples)
     normed = normed.transpose(0, 3, 1, 2, 4).reshape(pairs * channels, PAIR * events, samples)
 
-    steps = pairs // 2
-    onehot = (station_group[:, None] == jnp.arange(GROUPS, dtype=jnp.int32)[None, :]).astype(
-        jnp.float32
-    )
-    coef = onehot.reshape(2, steps, PAIR, GROUPS).transpose(1, 3, 0, 2)
-    coef = jnp.broadcast_to(
-        coef[:, :, :, None, :, None], (steps, GROUPS, 2, slots, PAIR, events)
-    ).reshape(steps, GROUPS, 2 * slots * PAIR * events)
-    members = jnp.pad(onehot.T, ((0, 0), (0, -stations % 128)))
-    member = (members[:, None, :] * flags[None]).reshape(GROUPS * events, -1)
-    highest = peaks(owners, normed, flags, coef, member, tiles // 2, parts, samples)
+    members = jnp.broadcast_to(jnp.pad(station_group, (0, -stations % 128))[None], flags.shape)
+    highest = peaks(owners, station_group, normed, flags, members, tiles // 2, parts, samples)
     highest = highest.reshape(GROUPS, events, 2, slots, PAIR, events)[:, :, 0, :, 0, :]
     return highest.reshape(GROUPS, events, slots * events).transpose(0, 2, 1)
 

time: 90.3 us -> 86.5 us (0.958)
  Pallas kernels: 81.4 us -> 78.7 us
    pallas_call x1, Pallas kernels: 81.4 us -> 78.7 us  [peaks(): pl.pallas_call(functools.partial(peak_kernel, line, parts, slots, float(s...]
    reshape x1 -> x0, local copies, waits for them, and re-layouts: 1.32 us -> none  [shards(): coef = jnp.broadcast_to(coef[:, :, :, None, :, None], (steps, GROUPS, 2,...]
where the time goes in v4:
time: 86.5 us; the launch traced here: 86.3 us
  Pallas kernels  78.7 us (91%)
  local copies, waits for them, and re-layouts  5.08 us (6%)
  other arithmetic  2.45 us (3%)
    pallas_call x1, Pallas kernels, peaks(): pl.pallas_call(functools.partial(peak_kernel, line, parts, slots, float(s...  78.7 us

profile of v4, /device:TPU:0, one launch (start us, length us, event | category | flops | bytes accessed | tf_op | source)
XLA Modules:
  0.0 86.3 jit_solution(3641396126197027834)
XLA Ops:
  0.0 0.0 copy-start
  0.0 0.8 convert_bitcast_fusion
  0.8 0.1 copy.12
  0.8 1.4 %fusion = f32[32,8,3]{1,2,0:T(4,128)S(1)} fusion(bf16[32,8,3,512]{3,1,2,0:T(8,128)(2,1)} %param.4), kind=kLoop, calls=%fused_computation.2 | loop fusion | flops 1178880 | bytes 789504 | tf_op jit(solution)/shard_map/reduce_sum | solution.py:23
  2.2 0.1 copy.10
  2.3 0.1 copy.11
  2.4 0.0 copy-done
  2.4 0.3 fusion.2
  2.7 0.0 copy-start.1
  2.7 1.0 %copy.13 = bf16[16,2,8,3,512]{4,2,1,3,0:T(8,128)(2,1)} copy(bf16[16,2,8,3,512]{4,2,3,1,0:T(8,128)(2,1)S(1)} %bitcast.8) | data formatting | bytes 1572864 | tf_op jit(solution)/shard_map/reshape | solution.py:396
  3.7 0.6 pad.8.flags_ref
  4.3 0.0 copy-done.1
  4.3 0.6 broadcast_in_dim.2.member_ref
  4.9 78.7 %shard_map.46 = f32[8,8,128]{2,1,0:T(8,128)} custom-call(s32[4]{0:T(128)} %owners_ref.1, s32[32]{0:T(128)} %group_ref.1, bf16[48,16,512]{2,1,0:T(8,128)(2,1)} %bitcast.7, f32[8,128]{1,0:T(8,128)} %pad.8.flags_ref, s32[8,128]{1,0:T(8,128)} %broadcast_in_dim.2.member_ref), custom_call_target="tpu_custom_call" | custom-call | tf_op jit(solution)/shard_map/pallas_call | solution.py:363
  83.6 1.6 %reshape.22 = f32[8,8,2,4,2,8]{5,4,3,2,1,0:T(2,128)S(1)} reshape(f32[8,8,128]{2,1,0:T(8,128)} %shard_map.46) | data formatting | bytes 65536 | tf_op jit(solution)/shard_map/reshape | solution.py:401
  85.1 0.4 slice_reduce_fusion
  85.5 0.7 reshape_squeeze.3
  (2 shorter events, 0.0 us)
Async XLA Ops:
  0.0 2.4 %copy-start = (bf16[32,8,3,512]{3,1,2,0:T(8,128)(2,1)S(1)}, bf16[32,8,3,512]{3,1,2,0:T(8,128)(2,1)}, u32[]{:S(2)}) copy-start(bf16[32,8,3,512]{3,1,2,0:T(8,128)(2,1)} %param.4) | copy-start | bytes 2359300
  2.7 1.6 %copy-start.1 = (s32[32]{0:T(128)S(1)}, s32[32]{0:T(128)}, u32[]{:S(2)}) copy-start(s32[32]{0:T(128)} %group_ref.1) | copy-start | bytes 388

commit v5 on v4

--- a/solution.py
+++ b/solution.py
@@ -29,7 +29,7 @@
 def peak_kernel(
     line, parts, slots, samples,
     owners_ref, group_ref, mine_ref, flags_ref, member_ref, peak_ref,
-    out_ref, everyone_ref, shifted, products, total, part, landed, common_ref, counted,
+    out_ref, everyone_ref, shifted, products, total, part, landed, common_ref, counted, gathered,
     beside, up_out, up_in, down_out, down_in,
     beside_send, beside_recv, up_send, up_recv, down_send, down_recv, out_send, out_recv,
     flags_send, flags_recv, flags_local,
@@ -324,14 +324,14 @@
             flag, pltpu.roll(highest, events, axis=1), pltpu.roll(highest, columns - events, axis=1)
         ),
     )
-    peak_ref[pl.ds(sta * share, share)] = highest.reshape(share, events, columns) / (
+    gathered[pl.ds(sta * share, share)] = highest.reshape(share, events, columns) / (
         samples * jnp.maximum(common, 1.0)
     )
     backs = []
     for hop in range(1, parts):
         mine = pl.ds(sta * share, share)
         copy = pltpu.make_async_remote_copy(
-            src_ref=peak_ref.at[mine], dst_ref=peak_ref.at[mine],
+            src_ref=gathered.at[mine], dst_ref=gathered.at[mine],
             send_sem=back_send.at[hop - 1], recv_sem=back_recv.at[hop - 1],
             device_id=(tile, lax.rem(sta + hop, parts)), device_id_type=MESH,
         )
@@ -343,10 +343,16 @@
         backs[hop - 1].wait_send()
         theirs = pl.ds(lax.rem(sta + parts - hop, parts) * share, share)
         pltpu.make_async_remote_copy(
-            src_ref=peak_ref.at[theirs], dst_ref=peak_ref.at[theirs],
+            src_ref=gathered.at[theirs], dst_ref=gathered.at[theirs],
             send_sem=back_send.at[hop - 1], recv_sem=back_recv.at[hop - 1],
             device_id=(tile, lax.rem(sta + hop, parts)), device_id_type=MESH,
         ).wait_recv()
+    for group in range(GROUPS):
+        turned = jnp.transpose(gathered[group])
+        for slot in range(slots):
+            peak_ref[group, pl.ds(slot * events, events)] = (
+                turned[slot * rows : slot * rows + events]
+            )
 
 
 def peaks(owners, station_group, blocks, flags, members, line, parts, samples):
@@ -362,7 +368,7 @@
     dma_sta = pltpu.SemaphoreType.DMA((parts - 1,))
     return pl.pallas_call(
         functools.partial(peak_kernel, line, parts, slots, float(samples)),
-        out_shape=jax.ShapeDtypeStruct((GROUPS, events, columns), jnp.float32),
+        out_shape=jax.ShapeDtypeStruct((GROUPS, slots * events, events), jnp.float32),
         in_specs=[pl.BlockSpec(memory_space=pltpu.SMEM)] * 2
         + [pl.BlockSpec(memory_space=pltpu.VMEM)] * 3,
         out_specs=pl.BlockSpec(memory_space=pltpu.VMEM),
@@ -376,6 +382,7 @@
             pltpu.VMEM((parts - 1, share, LAGS // 4, events, columns), jnp.float32),
             pltpu.VMEM((GROUPS, events, columns), jnp.float32),
             pltpu.VMEM((parts - 1, share, events, columns), jnp.float32),
+            pltpu.VMEM((GROUPS, events, columns), jnp.float32),
             pltpu.VMEM((steps, CHUNK, rows, width), blocks.dtype), store, store, store, store,
         ]
         + [dma] * 8
@@ -397,9 +404,9 @@
     normed = normed.transpose(0, 3, 1, 2, 4).reshape(pairs * channels, PAIR * events, samples)
 
     members = jnp.broadcast_to(jnp.pad(station_group, (0, -stations % 128))[None], flags.shape)
-    highest = peaks(owners, station_group, normed, flags, members, tiles // 2, parts, samples)
-    highest = highest.reshape(GROUPS, events, 2, slots, PAIR, events)[:, :, 0, :, 0, :]
-    return highest.reshape(GROUPS, events, slots * events).transpose(0, 2, 1)
+    return peaks(
+        owners, station_group, normed, flags, members, tiles // 2, parts, samples
+    )
 
 
 def solution(mesh):

time: 86.5 us -> 85.6 us (0.990)
  local copies, waits for them, and re-layouts: 5.08 us -> 4.03 us
    pallas_call x0 -> x1, local copies, waits for them, and re-layouts: none -> 1.61 us  [peaks(): pl.pallas_call(functools.partial(peak_kernel, line, parts, slots, float(s...]
    reshape x1 -> x0, local copies, waits for them, and re-layouts: 1.56 us -> none  [shards(): highest.reshape(GROUPS, events, 2, slots, PAIR, events)[:, :, 0, :, 0, :]]
where the time goes in v5:
time: 85.6 us; the launch traced here: 85.4 us
  Pallas kernels  78.9 us (92%)
  local copies, waits for them, and re-layouts  4.03 us (5%)
  other arithmetic  2.45 us (3%)
    pallas_call x1, Pallas kernels, peaks(): pl.pallas_call(functools.partial(peak_kernel, line, parts, slots, float(s...  78.9 us

profile of v5, /device:TPU:0, one launch (start us, length us, event | category | flops | bytes accessed | tf_op | source)
XLA Modules:
  0.0 85.4 jit_solution(4147333203461781749)
XLA Ops:
  0.0 0.0 copy-start
  0.0 0.8 convert_bitcast_fusion
  0.8 0.1 copy.14
  0.8 1.4 %fusion = f32[32,8,3]{1,2,0:T(4,128)S(1)} fusion(bf16[32,8,3,512]{3,1,2,0:T(8,128)(2,1)} %param.4), kind=kLoop, calls=%fused_computation.2 | loop fusion | flops 1178880 | bytes 789504 | tf_op jit(solution)/shard_map/reduce_sum | solution.py:23
  2.2 0.1 copy.12
  2.3 0.1 copy.13
  2.4 0.0 copy-done
  2.4 0.3 fusion.2
  2.7 0.0 copy-start.1
  2.7 1.0 %copy.15 = bf16[16,2,8,3,512]{4,2,1,3,0:T(8,128)(2,1)} copy(bf16[16,2,8,3,512]{4,2,3,1,0:T(8,128)(2,1)S(1)} %bitcast.7) | data formatting | bytes 1572864 | tf_op jit(solution)/shard_map/reshape | solution.py:403
  3.7 0.6 pad.8.flags_ref
  4.3 0.0 copy-done.1
  4.3 0.6 broadcast_in_dim.2.member_ref
  4.9 78.9 %shard_map.46 = f32[8,32,8]{2,1,0:T(8,128)} custom-call(s32[4]{0:T(128)} %owners_ref.1, s32[32]{0:T(128)} %group_ref.1, bf16[48,16,512]{2,1,0:T(8,128)(2,1)} %bitcast.6, f32[8,128]{1,0:T(8,128)} %pad.8.flags_ref, s32[8,128]{1,0:T(8,128)} %broadcast_in_dim.2.member_ref), custom_call_target="tpu_custom_call" | custom-call | tf_op jit(solution)/shard_map/pallas_call | solution.py:369
  83.8 1.6 %copy.16 = f32[8,32,8]{1,2,0:T(8,128)} copy(f32[8,32,8]{2,1,0:T(8,128)} %shard_map.46) | data formatting | bytes 16384 | tf_op jit(solution)/shard_map/pallas_call | solution.py:369
  (2 shorter events, 0.0 us)
Async XLA Ops:
  0.0 2.4 %copy-start = (bf16[32,8,3,512]{3,1,2,0:T(8,128)(2,1)S(1)}, bf16[32,8,3,512]{3,1,2,0:T(8,128)(2,1)}, u32[]{:S(2)}) copy-start(bf16[32,8,3,512]{3,1,2,0:T(8,128)(2,1)} %param.4) | copy-start | bytes 2359300
  2.7 1.6 %copy-start.1 = (s32[32]{0:T(128)S(1)}, s32[32]{0:T(128)}, u32[]{:S(2)}) copy-start(s32[32]{0:T(128)} %group_ref.1) | copy-start | bytes 388
